TPU v7x, 32 devices: a whole 2x2x4 slice. The times are simulated.
32 devices in a mesh: expert: 8 (over z, x), tensor: 4 (over y, core).
Axes of the slice: x: 2, y: 2, z: 4, core: 2. Of those that a mesh axis runs over, the one named last changes fastest.
Arguments:
- attn_vals: bfloat16 [512, 4096], P('expert', 'tensor'), may hold values from -6 to 6
- residual: bfloat16 [512, 4096], P('expert', 'tensor'), may hold values from -6 to 6
- out_weight: bfloat16 [4096, 4096], P('tensor'), may hold values from -0.09375 to 0.09375
- norm_gain: float32 [4096], P('tensor'), may hold values from 0.5 to 1.5
- router_weight: float32 [4096, 8], P('tensor'), may hold values from -0.09375 to 0.09375
- routes: int32 [512, 2], P('expert'), may hold values from 0 to 7, all different within a row; in each aligned block of 64 rows (0 to 63, 64 to 127, ...) at most 32 rows name the same one
- w_gate: bfloat16 [8, 4096, 8192], P('expert', None, 'tensor'), may hold values from -0.09375 to 0.09375
- w_up: bfloat16 [8, 4096, 8192], P('expert', None, 'tensor'), may hold values from -0.09375 to 0.09375
- w_down: bfloat16 [8, 8192, 4096], P('expert', 'tensor'), may hold values from -0.0625 to 0.0625
- slab_of: int32 [8], replicated, may hold values from 0 to 7, each once
- final_gain: float32 [4096], P('tensor'), may hold values from 0.5 to 1.5
- row_order: int32 [512], replicated, may hold values from 0 to 511, each once
Outputs:
- stream_out: bfloat16 [512, 4096], P('expert', 'tensor')
- normed_out: bfloat16 [512, 4096], P('expert', 'tensor')
Inputs may be any that keep to these rules, and one draw needn't show every extreme that they name: `routes`: the two experts of a row differ. In each aligned block of 64 rows (the rows of one device) no expert is named by more than 32 rows, and some block names one expert exactly 32 times. `slab_of`: A permutation. `row_order`: A permutation.
All inputs are finite; a program needn't handle non-finite values.
Results may differ from a plain program's by a relative error of at most 0.017.
Values may be sent and summed in bfloat16 or wider, within the bound.
A program may use at most 128 MiB of HBM per device.

v0:
```python
import jax
import jax.numpy as jnp
from jax import lax
from jax.sharding import PartitionSpec as P

D = 4096
MOST = 32


EPS = 1e-05


def finish_slots(gate_val, up_val, down_weight):
    active = (jax.nn.silu(gate_val) * up_val).astype(jnp.bfloat16)
    partial_out = jnp.einsum("gmf,fd->gmd", active, down_weight, preferred_element_type=jnp.float32)
    summed = lax.psum_scatter(
        partial_out.astype(jnp.bfloat16), "tensor", scatter_dimension=2, tiled=True
    )
    return lax.all_to_all(summed, "expert", split_axis=0, concat_axis=0, tiled=True)


def final_norm(stream, final_gain):
    stream_f = stream.astype(jnp.float32)
    square_total = lax.psum(jnp.sum(stream_f * stream_f, axis=1), "tensor")
    factor = lax.rsqrt(square_total / D + EPS)
    return (stream_f * factor[:, None] * final_gain).astype(jnp.bfloat16)


def on_device(
    attn_vals,
    residual,
    out_weight,
    norm_gain,
    router_weight,
    routes,
    w_gate,
    w_up,
    w_down,
    slab_of,
    final_gain,
    row_order,
):
    groups = lax.axis_size("expert")
    row_count = attn_vals.shape[0]
    expert_count = router_weight.shape[1]
    slab_count = groups // expert_count
    partial_proj = jnp.dot(attn_vals, out_weight, preferred_element_type=jnp.float32)
    project = lax.psum_scatter(
        partial_proj.astype(jnp.bfloat16), "tensor", scatter_dimension=1, tiled=True
    ).astype(jnp.float32)
    stream_in = (residual.astype(jnp.float32) + project).astype(jnp.bfloat16)
    hidden_f = stream_in.astype(jnp.float32)
    scaled = hidden_f * norm_gain
    square_sum, logit_part = lax.psum(
        (
            jnp.sum(hidden_f * hidden_f, axis=1),
            jnp.dot(scaled, router_weight, precision=lax.Precision.HIGHEST),
        ),
        "tensor",
    )
    inverse_rms = lax.rsqrt(square_sum / D + EPS)
    normed_in = (scaled * inverse_rms[:, None]).astype(jnp.bfloat16)
    logits = logit_part * inverse_rms[:, None]
    expert_ids = jnp.arange(expert_count, dtype=jnp.int32)
    route_hot = (routes[:, :, None] == expert_ids[None, None, :]).astype(jnp.int32)
    chosen = jnp.sum(route_hot.astype(jnp.float32) * logits[:, None, :], axis=2)
    leading = jax.nn.sigmoid(chosen[:, 0] - chosen[:, 1])
    mixing = jnp.stack([leading, 1.0 - leading], axis=1)
    route_hits = jnp.sum(route_hot, axis=1)
    before_count = jnp.cumsum(route_hits, axis=0) - route_hits
    slot_ids = jnp.sum(route_hot * before_count[:, None, :], axis=2)
    slot_hot = (slot_ids[:, :, None] == jnp.arange(MOST, dtype=jnp.int32)[None, None, :]).astype(
        jnp.float32
    )
    placing = jnp.einsum("rke,rks->esr", route_hot.astype(jnp.float32), slot_hot).astype(
        jnp.bfloat16
    )
    target_expert = slab_of // slab_count
    send_map = jnp.take(placing, target_expert, axis=0)
    full_rows = lax.all_gather(normed_in, "tensor", axis=1, tiled=True)
    outgoing = jnp.einsum(
        "gsr,rd->gsd", send_map, full_rows, preferred_element_type=jnp.float32
    ).astype(jnp.bfloat16)
    arrived = lax.all_to_all(outgoing, "expert", split_axis=0, concat_axis=0, tiled=True)
    gate_val = jnp.einsum("gmd,df->gmf", arrived, w_gate[0], preferred_element_type=jnp.float32)
    up_val = jnp.einsum("gmd,df->gmf", arrived, w_up[0], preferred_element_type=jnp.float32)
    returned = finish_slots(gate_val, up_val, w_down[0])
    group_ids = jnp.arange(groups, dtype=jnp.int32)
    holder_hot = (slab_of[None, :] == group_ids[:, None]).astype(jnp.int32)
    holders = jnp.sum(holder_hot * group_ids[None, :], axis=1).reshape(expert_count, slab_count)
    row_holders = jnp.take(holders, routes, axis=0)
    flat_index = row_holders * MOST + slot_ids[:, :, None]
    flat_back = returned.reshape(groups * MOST, returned.shape[2])
    fetched = jnp.take(flat_back, flat_index.reshape(-1), axis=0).reshape(
        row_count, 2, slab_count, returned.shape[2]
    )
    expert_out = jnp.sum(fetched.astype(jnp.float32), axis=2)
    blended = jnp.sum(mixing[:, :, None] * expert_out, axis=1)
    stream = (hidden_f + blended).astype(jnp.bfloat16)
    positions = lax.axis_index("expert") * row_count + jnp.arange(row_count, dtype=jnp.int32)
    matches = (row_order[None, :] == positions[:, None]).astype(jnp.int32)
    source = jnp.sum(matches * jnp.arange(row_order.shape[0], dtype=jnp.int32)[None, :], axis=1)
    normed = final_norm(stream, final_gain)
    all_stream, all_normed = (
        lax.all_gather(stream, "expert", axis=0, tiled=True),
        lax.all_gather(normed, "expert", axis=0, tiled=True),
    )
    return (jnp.take(all_stream, source, axis=0), jnp.take(all_normed, source, axis=0))


def solution(mesh):
    return jax.shard_map(
        on_device,
        mesh=mesh,
        in_specs=(
            P("expert", "tensor"),
            P("expert", "tensor"),
            P("tensor", None),
            P("tensor"),
            P("tensor", None),
            P("expert", None),
            P("expert", None, "tensor"),
            P("expert", None, "tensor"),
            P("expert", "tensor", None),
            P(),
            P("tensor"),
            P(),
        ),
        out_specs=(P("expert", "tensor"), P("expert", "tensor")),
        check_vma=False,
    )
```

profile of v0, /device:TPU:0, one launch (start us, length us, event | category | flops | bytes accessed | tf_op | source)
XLA Modules:
  0.0 283.7 jit_solution(16492582065069274583)
XLA Ops:
  7.2 0.0 copy-start
  7.2 0.0 copy-start.7
  7.2 0.0 reduce-scatter.3.cloned.1.call-start
  7.2 0.8 copy-done
  8.1 5.7 %convolution_convert_fusion.1 = bf16[64,4096]{1,0:T(8,128)(2,1)} fusion(bf16[64,1024]{1,0:T(8,128)(2,1)S(1)} %copy-done, bf16[1024,4096]{1,0:T(8,128)(2,1)} %param.16), kind=kOutput, calls=%fused_computation.12 | convolution fusion | flops 537133056 | bytes 9043968 | tf_op jit(solution)/shard_map/dot_general | solution.py:47
  13.8 0.0 reduce-scatter.3.cloned.1.call-update
  13.9 0.0 reduce-scatter.5.cloned.1.call-start
  13.9 0.0 copy-done.7
  13.9 0.1 copy.50
  14.0 0.2 convert_reduce_fusion
  14.2 0.1 reduce_window_sum.11
  14.3 1.2 select_reduce_fusion.1
  15.5 0.4 fusion.17
  16.0 0.1 copy.57
  16.1 0.0 copy-done.9
  16.1 0.6 gather_fusion
  16.7 21.6 %reduce-scatter.3.cloned.1.call-done = bf16[64,1024]{1,0:T(8,128)(2,1)} async-done(((bf16[64,4096]{1,0:T(8,128)(2,1)}), bf16[64,1024]{1,0:T(8,128)(2,1)}) %reduce-scatter.3.cloned.1.call-update) | async-done | bytes 131088 | tf_op jit(solution)/shard_map/reduce_scatter | solution.py:48
  38.4 0.0 copy-done.3
  38.4 1.1 fusion.26
  39.4 0.0 copy-done.4
  39.4 0.0 copy-done.5
  39.4 0.3 fusion.21
  39.7 5.9 %all-reduce = (f32[64]{0:T(128)S(1)}, f32[64,8]{0,1:T(8,128)S(1)}) all-reduce(f32[64]{0:T(128)S(1)} %get-tuple-element.11, f32[64,8]{0,1:T(8,128)S(1)} %fusion.21), channel_id=1, replica_groups=mesh['expert'=8,'tensor'=4] {'tensor'}, use_global_device_ids=true, to_apply=%region_3.0 | all-reduce | flops 576 | bytes 4608 | tf_op jit(solution)/shard_map/psum | solution.py:54
  45.6 0.1 fusion.22
  45.7 7.4 %all_gather.9 = bf16[64,4096]{1,0:T(8,128)(2,1)S(1)} all-gather(bf16[64,1024]{1,0:T(8,128)(2,1)S(1)} %fusion.22), channel_id=1, replica_groups=mesh['expert'=8,'tensor'=4] {'tensor'}, dimensions={1}, use_global_device_ids=true | all-gather | bytes 655360 | tf_op jit(solution)/shard_map/all_gather | solution.py:80
  53.1 0.7 convolution_convert_fusion
  53.8 54.0 %all_to_all.10 = bf16[8,32,4096]{2,1,0:T(8,128)(2,1)S(1)} all-to-all(bf16[8,32,4096]{2,1,0:T(8,128)(2,1)S(1)} %convolution_convert_fusion), channel_id=1, replica_groups=mesh['expert'=8,'tensor'=4] {'expert'}, dimensions={0} | all-to-all | bytes 4194304 | tf_op jit(solution)/shard_map/all_to_all | solution.py:84
  107.8 9.4 %fusion.4 = f32[8,32,2048]{2,1,0:T(8,128)} fusion(bf16[8,32,4096]{2,1,0:T(8,128)(2,1)S(1)} %all_to_all.10, bf16[1,4096,2048]{2,1,0:T(8,128)(2,1)} %param.20), kind=kOutput, calls=%fused_computation.8 | convolution fusion | flops 4294967296 | bytes 20971520 | tf_op jit(solution)/shard_map/gmd,df->gmf/dot_general | solution.py:85
  117.2 17.4 %fusion.6 = bf16[8,32,4096]{2,1,0:T(8,128)(2,1)} fusion(bf16[1,2048,4096]{2,1,0:T(8,128)(2,1)} %param.22, bf16[8,32,4096]{2,1,0:T(8,128)(2,1)S(1)} %all_to_all.10, bf16[1,4096,2048]{2,1,0:T(8,128)(2,1)} %param.21, f32[8,32,2048]{2,1,0:T(8,128)} %fusion.4), kind=kOutput, calls=%fused_computation.11 | convolution fusion | flops 8594128896 | bytes 39845888 | tf_op jit(solution)/shard_map/gmf,fd->gmd/dot_general | solution.py:15
  134.7 0.0 reduce-scatter.5.cloned.1.call-update
  134.7 0.1 copy.55
  134.8 0.1 select_reduce_fusion.2
  134.9 0.7 fusion.46
  135.6 5.2 %compare_and_fusion.2 = (pred[64,2]{0,1:T(4,128)(4,1)S(1)}, s32[64,2]{0,1:T(2,128)S(1)}) fusion(s32[64,2]{0,1:T(2,128)S(1)} %copy.55, s32[]{:T(128)} %bitcast.7, s32[]{:T(128)} %bitcast.6, s32[]{:T(128)} %bitcast.5, s32[]{:T(128)} %bitcast.4, s32[]{:T(128)} %bitcast.3, s32[]{:T(128)} %bitcast.2, s32[]{:T(128)} %bitcast.1, s32[]{:T(128)} %bitcast, ...), kind=kLoop, calls=%fused_computation.72 | loop fusion | flops 3712 | bytes 1696 | tf_op jit(solution)/shard_map/jit(_take)/and | solution.py:94
  140.8 0.1 copy.58
  140.9 0.1 reshape.187
  141.0 23.7 %reduce-scatter.5.cloned.1.call-done = bf16[8,32,1024]{2,1,0:T(8,128)(2,1)} async-done(((bf16[8,32,4096]{2,1,0:T(8,128)(2,1)}), bf16[8,32,1024]{2,1,0:T(8,128)(2,1)}) %reduce-scatter.5.cloned.1.call-update) | async-done | bytes 524304 | tf_op jit(solution)/shard_map/reduce_scatter | solution.py:16
  164.7 5.5 %all-to-all-start.1 = ((bf16[8,32,1024]{2,1,0:T(8,128)(2,1)}), bf16[8,32,1024]{2,1,0:T(8,128)(2,1)S(1)}, u32[]{:S(2)}, u32[]{:S(2)}) async-start(bf16[8,32,1024]{2,1,0:T(8,128)(2,1)} %reduce-scatter.5.cloned.1.call-done), calls=%async_computation.3 | async-start | bytes 1048576 | tf_op jit(solution)/shard_map/all_to_all | solution.py:19
  170.2 0.2 all-gather.5.cloned.1.call-start
  170.4 0.1 copy.56
  170.5 0.1 copy.51
  170.6 0.2 fusion.31
  170.8 0.0 copy-start.6
  170.9 0.1 fusion.45
  170.9 0.1 copy.59
  171.0 0.1 copy.60
  171.1 0.1 copy.54
  171.2 13.5 %all-to-all-done.1 = bf16[8,32,1024]{2,1,0:T(8,128)(2,1)S(1)} async-done(((bf16[8,32,1024]{2,1,0:T(8,128)(2,1)}), bf16[8,32,1024]{2,1,0:T(8,128)(2,1)S(1)}, u32[]{:S(2)}, u32[]{:S(2)}) %all-to-all-start.1) | async-done | bytes 524320 | tf_op jit(solution)/shard_map/all_to_all | solution.py:19
  184.7 0.9 gather_fusion.1
  185.5 0.1 gather.26
  185.6 0.0 copy-start.1
  185.7 0.9 multiply_reduce_fusion
  186.5 0.1 fusion.23
  186.7 5.9 %psum.23 = f32[64]{0:T(128)S(1)} all-reduce(f32[64]{0:T(128)S(1)} %get-tuple-element.5), channel_id=1, replica_groups=mesh['expert'=8,'tensor'=4] {'tensor'}, use_global_device_ids=true, to_apply=%region_13.15 | all-reduce | flops 64 | bytes 512 | tf_op jit(solution)/shard_map/psum | solution.py:24
  192.6 0.8 fusion.25
  193.4 0.0 all-gather.5.cloned.1.call-update
  193.4 0.0 all-gather.3.cloned.1.call-start
  193.5 0.5 all-gather.3.cloned.1.call-update
  194.0 0.2 select_reduce_fusion
  194.2 38.5 %all-gather.5.cloned.1.call-done = bf16[512,1024]{1,0:T(8,128)(2,1)} async-done(((bf16[64,1024]{1,0:T(8,128)(2,1)}), bf16[512,1024]{1,0:T(8,128)(2,1)}) %all-gather.5.cloned.1.call-update) | async-done | bytes 1048592 | tf_op jit(solution)/shard_map/all_gather | solution.py:106
  232.7 2.2 gather_fusion.3
  234.9 39.3 %all-gather.3.cloned.1.call-done = bf16[512,1024]{1,0:T(8,128)(2,1)} async-done(((bf16[64,1024]{1,0:T(8,128)(2,1)}), bf16[512,1024]{1,0:T(8,128)(2,1)}) %all-gather.3.cloned.1.call-update) | async-done | bytes 1048592 | tf_op jit(solution)/shard_map/all_gather | solution.py:105
  274.2 2.2 gather_fusion.2
  276.4 0.8 broadcast_select_fusion.1
  (25 shorter events, 0.1 us)
Async XLA Ops:
  7.2 0.9 copy-start
  7.2 6.7 %copy-start.7 = (s32[64,2]{0,1:T(2,128)S(1)}, s32[64,2]{0,1:T(2,128)}, u32[]{:S(2)}) copy-start(s32[64,2]{0,1:T(2,128)} %param.19) | copy-start | bytes 1540
  7.2 31.2 %reduce-scatter.3.cloned.1.call-start = ((), (), s32[]{:S(2)}) async-start(), calls=%async_computation.4 | async-start | bytes 655360 | tf_op jit(solution)/shard_map/reduce_scatter | solution.py:48
  13.8 2.3 copy-start.9
  13.8 24.6 %copy-start.3 = (bf16[64,1024]{1,0:T(8,128)(2,1)S(1)}, bf16[64,1024]{1,0:T(8,128)(2,1)}, u32[]{:S(2)}) copy-start(bf16[64,1024]{1,0:T(8,128)(2,1)} %param.15) | copy-start | bytes 393220
  13.8 25.6 %copy-start.4 = (f32[1024,8]{0,1:T(8,128)S(1)}, f32[1024,8]{0,1:T(8,128)}, u32[]{:S(2)}) copy-start(f32[1024,8]{0,1:T(8,128)} %param.18) | copy-start | bytes 98308
  13.8 25.6 %copy-start.5 = (f32[1024]{0:T(1024)S(1)}, f32[1024]{0:T(1024)}, u32[]{:S(2)}) copy-start(f32[1024]{0:T(1024)} %param.17) | copy-start | bytes 12292
  13.9 150.8 %reduce-scatter.5.cloned.1.call-start = ((), (), s32[]{:S(2)}) async-start(), calls=%async_computation.5 | async-start | bytes 2621440 | tf_op jit(solution)/shard_map/reduce_scatter | solution.py:16
  164.7 20.0 %all-to-all-start.1 = ((bf16[8,32,1024]{2,1,0:T(8,128)(2,1)}), bf16[8,32,1024]{2,1,0:T(8,128)(2,1)S(1)}, u32[]{:S(2)}, u32[]{:S(2)}) async-start(bf16[8,32,1024]{2,1,0:T(8,128)(2,1)} %reduce-scatter.5.cloned.1.call-done), calls=%async_computation.3 | async-start | bytes 1048576 | tf_op jit(solution)/shard_map/all_to_all | solution.py:19
  170.2 62.6 %all-gather.5.cloned.1.call-start = ((), (), s32[]{:S(2)}) async-start(), calls=%async_computation.7 | async-start | bytes 1179648 | tf_op jit(solution)/shard_map/all_gather | solution.py:106
  170.8 21.8 %copy-start.6 = (f32[1024]{0:T(1024)S(1)}, f32[1024]{0:T(1024)}, u32[]{:S(2)}) copy-start(f32[1024]{0:T(1024)} %param.24) | copy-start | bytes 12292
  184.7 9.3 %copy-start.8 = (s32[512]{0:T(512)S(1)}, s32[512]{0:T(512)}, u32[]{:S(2)}) copy-start(s32[512]{0:T(512)} %param.25) | copy-start | bytes 6148
  185.6 91.6 %copy-start.1 = (bf16[64,1024]{1,0:T(8,128)(2,1)S(1)}, bf16[64,1024]{1,0:T(8,128)(2,1)}, u32[]{:S(2)}) copy-start(bf16[64,1024]{1,0:T(8,128)(2,1)} %param.14) | copy-start | bytes 393220
  186.7 6.8 %copy-start.2 = (bf16[64,1024]{1,0:T(8,128)(2,1)}, bf16[64,1024]{1,0:T(8,128)(2,1)S(1)}, u32[]{:S(2)}) copy-start(bf16[64,1024]{1,0:T(8,128)(2,1)S(1)} %get-tuple-element.6) | copy-start | bytes 393220
  193.4 80.8 %all-gather.3.cloned.1.call-start = ((), (), s32[]{:S(2)}) async-start(), calls=%async_computation.6 | async-start | bytes 1179648 | tf_op jit(solution)/shard_map/all_gather | solution.py:105
Sparse Core Ops, SparseCore 0:
  14.0 24.3 reduce-scatter.2
  134.8 29.8 reduce-scatter.4
  193.5 39.1 all-gather.4
  235.3 38.9 all-gather.2
where the time goes:
time: 284 us
  waiting for transfers between devices  137 us (48%)
  blocking collectives  73.2 us (26%)
  matrix products  34 us (12%)
  between operations  14 us (5%)
  other arithmetic  11 us (4%)
  local copies, waits for them, and re-layouts  8.47 us (3%)
  starting transfers between devices  5.82 us (2%)
    all_to_all x1, blocking collectives, on_device(): lax.all_to_all(outgoing, 'expert', split_axis=0, concat_axis=0, tiled=True)  54 us
    all_gather x1, waiting for transfers between devices, on_device(): lax.all_gather(stream, 'expert', axis=0, tiled=True)  39.3 us
    all_gather x1, waiting for transfers between devices, on_device(): lax.all_gather(normed, 'expert', axis=0, tiled=True)  38.5 us
    reduce_scatter x1, waiting for transfers between devices, finish_slots(): lax.psum_scatter(partial_out.astype(jnp.bfloat16), 'tensor', scatter_dime...  23.7 us
    reduce_scatter x1, waiting for transfers between devices, on_device(): lax.psum_scatter(partial_proj.astype(jnp.bfloat16), 'tensor', scatter_dim...  21.6 us
    dot_general x1, matrix products, finish_slots(): jnp.einsum('gmf,fd->gmd', active, down_weight, preferred_element_type=jnp...  17.4 us
    all_to_all x1, waiting for transfers between devices, finish_slots(): lax.all_to_all(summed, 'expert', split_axis=0, concat_axis=0, tiled=True)  13.5 us
    dot_general x1, matrix products, on_device(): jnp.einsum('gmd,df->gmf', arrived, w_gate[0], preferred_element_type=jnp....  9.41 us
  transfers between devices with their start and end apart: 5, of which 5 were waited for; matrix products, arithmetic and copies ran while one was open for 4% of the time, Pallas kernels for 0%

commit v1 on v0

v1 whole, which is shorter than its diff:
```python
import functools

import jax
import jax.numpy as jnp
from jax import lax
from jax.experimental import pallas as pl
from jax.experimental.pallas import tpu as pltpu
from jax.sharding import PartitionSpec as P

MOST = 32
EPS = 1e-05
BF = jnp.bfloat16
F32 = jnp.float32


def dot(a, b):
    return jnp.dot(a, b, preferred_element_type=F32)


def layer_kernel(
    groups,
    parts,
    attn,
    residual,
    out_w,
    gain,
    router,
    routes,
    w_gate,
    w_up,
    w_down,
    slots,
    final_gain,
    order,
    stream_out,
    normed_out,
    ow,
    wg,
    wu,
    wd,
    proj_send,
    proj_recv,
    stat_send,
    stat_recv,
    out_rows,
    arr,
    act,
    part,
    sib,
    cross_send,
    cross_recv,
    slab,
    ret,
    all_stream,
    sq_send,
    sq_recv,
    w_sem,
    send_sem,
    recv_sem,
):
    e = lax.axis_index("expert")
    t = lax.axis_index("tensor")
    ny = parts // 2
    y, c = t // 2, t % 2
    rows, dl = residual.shape
    d_model = dl * parts
    count = router.shape[1]
    fl = act.shape[1]
    half = fl // 2
    slots_all = groups * MOST

    def part_of(yo, co, sign):
        core = c if co == 0 else 1 - c
        return lax.rem(y + sign * yo + ny, ny) * 2 + core

    used = [0]

    def remote(src, dst, dev):
        k = used[0]
        used[0] += 1
        return pltpu.make_async_remote_copy(
            src_ref=src,
            dst_ref=dst,
            send_sem=send_sem.at[k],
            recv_sem=recv_sem.at[k],
            device_id=dev,
            device_id_type=pl.DeviceIdType.MESH,
        )

    def at_part(j, sign=1):
        return (e, part_of(j // 2, j % 2, sign))

    def at_group(o, sign=1):
        return (lax.rem(e + sign * o + groups, groups), t)

    ow_copies = []
    for n, j in enumerate(list(range(1, parts)) + [0]):
        col = pl.multiple_of(part_of(j // 2, j % 2, 1) * dl, dl)
        cp = pltpu.make_async_copy(out_w.at[:, pl.ds(col, dl)], ow.at[j], w_sem.at[n])
        cp.start()
        ow_copies.append(cp)

    barrier = pltpu.get_barrier_semaphore()
    for j in range(1, parts):
        pl.semaphore_signal(barrier, inc=1, device_id=at_part(j), device_id_type=pl.DeviceIdType.MESH)
    for o in range(1, groups):
        pl.semaphore_signal(barrier, inc=1, device_id=at_group(o), device_id_type=pl.DeviceIdType.MESH)
    pl.semaphore_wait(barrier, parts + groups - 2)

    proj_copies = []
    own = None
    for n, j in enumerate(list(range(1, parts)) + [0]):
        ow_copies[n].wait()
        value = dot(attn[...], ow[j])
        if j:
            proj_send[j - 1] = value.astype(BF)
            cp = remote(proj_send.at[j - 1], proj_recv.at[j - 1], at_part(j))
            cp.start()
            proj_copies.append(cp)
        else:
            own = value.astype(BF).astype(F32)

    gu_copies, wd_copies = [], []
    n = parts
    for j in range(parts):
        row = pl.multiple_of(part_of(j // 2, j % 2, -1) * dl, dl)
        for src, dst in ((w_gate, wg), (w_up, wu)):
            cp = pltpu.make_async_copy(src.at[0, pl.ds(row, dl), :], dst.at[j], w_sem.at[n])
            cp.start()
            gu_copies.append(cp)
            n += 1
    for j in range(parts):
        col = pl.multiple_of(part_of(j // 2, j % 2, 1) * dl, dl)
        for k, dst in ((0, wd.at[j]), (1, ow.at[j, pl.ds(0, half), :])):
            cp = pltpu.make_async_copy(
                w_down.at[0, pl.ds(k * half, half), pl.ds(col, dl)], dst, w_sem.at[n]
            )
            cp.start()
            wd_copies.append(cp)
            n += 1

    route_f = routes[...].astype(F32)
    ids = lax.broadcasted_iota(jnp.int32, (rows, count), 1).astype(F32)
    hot = [jnp.where(route_f[:, k : k + 1] == ids, 1.0, 0.0) for k in range(2)]
    ri = lax.broadcasted_iota(jnp.int32, (rows, rows), 0)
    ci = lax.broadcasted_iota(jnp.int32, (rows, rows), 1)
    lower = jnp.where(ci < ri, 1.0, 0.0).astype(BF)
    before = dot(lower, (hot[0] + hot[1]).astype(BF))
    sel = []
    for k in range(2):
        place = jnp.sum(hot[k] * before, axis=1, keepdims=True)
        hit = jnp.where(slots[0:1, :] == route_f[:, k : k + 1], 1.0, 0.0)
        fit = jnp.where(slots[1:2, :] == place, 1.0, 0.0)
        sel.append(hit * fit)
    placing = (sel[0] + sel[1]).astype(BF)
    sel = [s.astype(BF) for s in sel]

    for cp in proj_copies:
        cp.wait_recv()
    for j in range(parts - 1):
        own = own + proj_recv[j].astype(F32)
    own = own.astype(BF).astype(F32)
    hidden = (residual[...].astype(F32) + own).astype(BF).astype(F32)
    scaled = hidden * gain[...]
    stat_send[...] = jnp.zeros_like(stat_send)
    stat_send[:, 0:count] = jnp.dot(
        scaled, router[...], precision=lax.Precision.HIGHEST, preferred_element_type=F32
    )
    stat_send[:, count : count + 1] = jnp.sum(hidden * hidden, axis=1, keepdims=True)
    stat_copies = []
    for j in range(1, parts):
        cp = remote(stat_send, stat_recv.at[j - 1], at_part(j))
        cp.start()
        stat_copies.append(cp)
    stats = stat_send[...]
    for cp in stat_copies:
        cp.wait_recv()
    for j in range(parts - 1):
        stats = stats + stat_recv[j]
    inverse = lax.rsqrt(stats[:, count : count + 1] / d_model + EPS)
    normed_in = (scaled * inverse).astype(BF)
    logits = stats[:, 0:count] * inverse
    chosen = [jnp.sum(hot[k] * logits, axis=1, keepdims=True) for k in range(2)]
    first = 1.0 / (1.0 + jnp.exp(chosen[1] - chosen[0]))
    mixing = [first, 1.0 - first]

    out_rows[...] = lax.dot_general(
        placing, normed_in, (((0,), (0,)), ((), ())), preferred_element_type=F32
    ).astype(BF)
    out_copies = []
    for o in range(1, groups):
        part_rows = pl.ds(o * MOST, MOST)
        cp = remote(out_rows.at[part_rows], arr.at[0, part_rows], at_group(o))
        cp.start()
        out_copies.append(cp)
    arr[0, 0:MOST] = out_rows[0:MOST]
    for cp in out_copies:
        cp.wait_recv()

    spread = [remote(arr.at[0], arr.at[2 * yo], at_part(2 * yo)) for yo in range(1, ny)]
    spread_sib = remote(arr.at[0], arr.at[1], at_part(1))
    for cp in spread:
        cp.start()
    spread_sib.start()
    passed = []
    for yo in range(1, ny):
        spread[yo - 1].wait_recv()
        cp = remote(arr.at[2 * yo], arr.at[2 * yo + 1], at_part(1))
        cp.start()
        passed.append(cp)
    spread_sib.wait_recv()
    for cp in passed:
        cp.wait_recv()
    for cp in gu_copies:
        cp.wait()

    rc = min(256, slots_all)
    fc = min(256, fl)

    @pl.loop(0, slots_all // rc)
    def _(r):
        rr = pl.ds(pl.multiple_of(r * rc, rc), rc)

        @pl.loop(0, fl // fc)
        def _(f):
            cc = pl.ds(pl.multiple_of(f * fc, fc), fc)
            gate = dot(arr[0, rr, :], wg[0, :, cc])
            up = dot(arr[0, rr, :], wu[0, :, cc])
            for j in range(1, parts):
                gate += dot(arr[j, rr, :], wg[j, :, cc])
                up += dot(arr[j, rr, :], wu[j, :, cc])
            act[rr, cc] = (gate / (1.0 + jnp.exp(-gate)) * up).astype(BF)

    for cp in wd_copies:
        cp.wait()
    dc = min(256, dl)

    def down(j):
        @pl.loop(0, slots_all // rc)
        def _(r):
            rr = pl.ds(pl.multiple_of(r * rc, rc), rc)

            @pl.loop(0, dl // dc)
            def _(f):
                cc = pl.ds(pl.multiple_of(f * dc, dc), dc)
                value = dot(act[rr, 0:half], wd[j, :, cc])
                value += dot(act[rr, half:fl], ow[j, 0:half, cc])
                part[j, rr, cc] = value.astype(BF)

    sib_copies = []
    yos = list(range(1, ny)) + [0]
    for yo in yos:
        down(2 * yo + 1)
        cp = remote(part.at[2 * yo + 1], sib.at[yo], at_part(1))
        cp.start()
        sib_copies.append(cp)
    cross = []
    for n, yo in enumerate(yos):
        down(2 * yo)
        sib_copies[n].wait_recv()
        if yo:
            cross_send[yo - 1] = (part[2 * yo].astype(F32) + sib[yo].astype(F32)).astype(BF)
            cp = remote(cross_send.at[yo - 1], cross_recv.at[yo - 1], at_part(2 * yo))
            cp.start()
            cross.append(cp)
    for cp in cross:
        cp.wait_recv()
    total = part[0].astype(F32) + sib[0].astype(F32)
    for yo in range(1, ny):
        total = total + cross_recv[yo - 1].astype(F32)
    slab[...] = total.astype(BF)

    back = []
    for o in range(1, groups):
        part_rows = pl.ds(o * MOST, MOST)
        cp = remote(slab.at[part_rows], ret.at[part_rows], at_group(o, -1))
        cp.start()
        back.append(cp)
    ret[0:MOST] = slab[0:MOST]
    for cp in back:
        cp.wait_recv()
    blended = mixing[0] * dot(sel[0], ret[...]) + mixing[1] * dot(sel[1], ret[...])
    all_stream[0:rows] = (hidden + blended).astype(BF)

    moved = []
    for o in range(1, groups):
        cp = remote(
            all_stream.at[pl.ds(0, rows)], all_stream.at[pl.ds(o * rows, rows)], at_group(o)
        )
        cp.start()
        moved.append(cp)
    want = lax.broadcasted_iota(jnp.int32, (rows, groups * rows), 0).astype(F32)
    pick = jnp.where(order[...] == want, 1.0, 0.0).astype(BF)
    for cp in moved:
        cp.wait_recv()
    stream = dot(pick, all_stream[...])
    stream_out[...] = stream.astype(BF)
    sq_send[...] = jnp.broadcast_to(jnp.sum(stream * stream, axis=1, keepdims=True), sq_send.shape)
    sq_copies = []
    for j in range(1, parts):
        cp = remote(sq_send, sq_recv.at[j - 1], at_part(j))
        cp.start()
        sq_copies.append(cp)
    square = sq_send[...]
    for cp in sq_copies:
        cp.wait_recv()
    for j in range(parts - 1):
        square = square + sq_recv[j]
    factor = lax.rsqrt(square[:, 0:1] / d_model + EPS)
    normed_out[...] = (stream * factor * final_gain[...]).astype(BF)

    started = proj_copies + stat_copies + out_copies + spread + [spread_sib] + passed
    for cp in started + sib_copies + cross + back + moved + sq_copies:
        cp.wait_send()


def on_device(
    attn_vals,
    residual,
    out_weight,
    norm_gain,
    router_weight,
    routes,
    w_gate,
    w_up,
    w_down,
    slab_of,
    final_gain,
    row_order,
):
    groups = lax.axis_size("expert")
    parts = lax.axis_size("tensor")
    ny = parts // 2
    e = lax.axis_index("expert")
    rows, dl = residual.shape
    d_model = out_weight.shape[1]
    slab_count = groups // router_weight.shape[1]
    fl = w_gate.shape[2]
    slots_all = groups * MOST
    steps = jnp.arange(groups, dtype=jnp.int32)
    held = jnp.take(slab_of // slab_count, (e + steps) % groups)
    slots = jnp.stack(
        [jnp.repeat(held, MOST), jnp.arange(slots_all, dtype=jnp.int32) % MOST]
    ).astype(F32)
    order = jnp.take(row_order.reshape(groups, rows), (e - steps) % groups, axis=0)
    order = (order.reshape(1, groups * rows) - e * rows).astype(F32)
    vmem = pl.BlockSpec(memory_space=pltpu.VMEM)
    hbm = pl.BlockSpec(memory_space=pl.ANY)
    copies = 3 * (parts - 1) + 3 * (groups - 1) + 2 * (ny - 1) + 1 + ny + ny - 1
    flops = 2 * (rows * dl * d_model + 3 * slots_all * d_model * fl)
    moved = 2 * (dl * d_model + 3 * d_model * fl)
    call = pl.pallas_call(
        functools.partial(layer_kernel, groups, parts),
        out_shape=[jax.ShapeDtypeStruct((rows, dl), BF)] * 2,
        in_specs=[vmem, vmem, hbm, vmem, vmem, vmem, hbm, hbm, hbm, vmem, vmem, vmem],
        out_specs=[vmem, vmem],
        scratch_shapes=[
            pltpu.VMEM((parts, dl, dl), BF),
            pltpu.VMEM((parts, dl, fl), BF),
            pltpu.VMEM((parts, dl, fl), BF),
            pltpu.VMEM((parts, fl // 2, dl), BF),
            pltpu.VMEM((parts - 1, rows, dl), BF),
            pltpu.VMEM((parts - 1, rows, dl), BF),
            pltpu.VMEM((rows, 128), F32),
            pltpu.VMEM((parts - 1, rows, 128), F32),
            pltpu.VMEM((slots_all, dl), BF),
            pltpu.VMEM((parts, slots_all, dl), BF),
            pltpu.VMEM((slots_all, fl), BF),
            pltpu.VMEM((parts, slots_all, dl), BF),
            pltpu.VMEM((ny, slots_all, dl), BF),
            pltpu.VMEM((max(ny - 1, 1), slots_all, dl), BF),
            pltpu.VMEM((max(ny - 1, 1), slots_all, dl), BF),
            pltpu.VMEM((slots_all, dl), BF),
            pltpu.VMEM((slots_all, dl), BF),
            pltpu.VMEM((groups * rows, dl), BF),
            pltpu.VMEM((rows, 128), F32),
            pltpu.VMEM((parts - 1, rows, 128), F32),
            pltpu.SemaphoreType.DMA((5 * parts,)),
            pltpu.SemaphoreType.DMA((copies,)),
            pltpu.SemaphoreType.DMA((copies,)),
        ],
        compiler_params=pltpu.CompilerParams(
            collective_id=0, has_side_effects=True, vmem_limit_bytes=62 * 2**20
        ),
        cost_estimate=pl.CostEstimate(flops=flops, bytes_accessed=moved, transcendentals=0),
    )
    return call(
        attn_vals,
        residual,
        out_weight,
        norm_gain.reshape(1, dl),
        router_weight,
        routes,
        w_gate,
        w_up,
        w_down,
        slots,
        final_gain.reshape(1, dl),
        order,
    )


def solution(mesh):
    return jax.shard_map(
        on_device,
        mesh=mesh,
        in_specs=(
            P("expert", "tensor"),
            P("expert", "tensor"),
            P("tensor", None),
            P("tensor"),
            P("tensor", None),
            P("expert", None),
            P("expert", None, "tensor"),
            P("expert", None, "tensor"),
            P("expert", "tensor", None),
            P(),
            P("tensor"),
            P(),
        ),
        out_specs=(P("expert", "tensor"), P("expert", "tensor")),
        check_vma=False,
    )
```

time: 284 us -> 132 us (0.46)
  the two profiles are of different devices: /device:TPU:0 before, /device:TPU:27 now
where the time goes in v1:
time: 132 us; the launch traced here: 131 us
  Pallas kernels  120 us (91%)
  local copies, waits for them, and re-layouts  9.61 us (7%)
    pallas_call x1, Pallas kernels, on_device(): call(attn_vals, residual, out_weight, norm_gain.reshape(1, dl), router_we...  120 us
    unnamed x6, local copies, waits for them, and re-layouts  6.86 us

profile of v1, /device:TPU:27, one launch (start us, length us, event | category | flops | bytes accessed | tf_op | source)
XLA Modules:
  0.0 131.4 jit_solution(15048430228911553207)
XLA Ops:
  0.6 0.0 copy-start
  0.7 0.6 copy-done
  1.3 0.6 gather_fusion
  2.0 0.1 broadcast_in_dim.15
  2.0 0.1 stack_reshape.3
  2.1 0.6 add_convert_fusion.slots
  2.7 0.8 reshape.179
  3.5 0.6 gather_fusion.1
  4.0 0.1 subtract_convert_fusion
  4.1 0.7 convert_element_type.10.order
  4.7 1.4 %copy.17.routes = s32[64,2]{1,0:T(8,128)} copy(s32[64,2]{0,1:T(2,128)} %param.17) | data formatting | bytes 1024 | tf_op args[5]
  6.1 1.8 %copy.16.router = f32[1024,8]{1,0:T(8,128)} copy(f32[1024,8]{0,1:T(8,128)} %param.16) | data formatting | bytes 65536 | tf_op args[4]
  7.9 120.4 %shard_map.131 = (bf16[64,1024]{1,0:T(8,128)(2,1)}, bf16[64,1024]{1,0:T(8,128)(2,1)}) custom-call(bf16[64,1024]{1,0:T(8,128)(2,1)} %attn.1, bf16[64,1024]{1,0:T(8,128)(2,1)} %residual.1, bf16[1024,4096]{1,0:T(8,128)(2,1)} %out_w.1, f32[1,1024]{1,0:T(1,128)} %bitcast.6, f32[1024,8]{1,0:T(8,128)} %copy.16.router, s32[64,2]{1,0:T(8,128)} %copy.17.routes, ...), custom_call_target="tpu_custom_call" | custom-call | flops 13421772800 | bytes 58720256 | tf_op jit(solution)/shard_map/pallas_call | solution.py:387
  128.3 1.6 %copy.20 = bf16[64,1024]{1,0:T(8,128)(2,1)} copy(bf16[64,1024]{1,0:T(8,128)(2,1)} %get-tuple-element.6) | data formatting | bytes 262144
  129.9 1.6 %copy.21 = bf16[64,1024]{1,0:T(8,128)(2,1)} copy(bf16[64,1024]{1,0:T(8,128)(2,1)} %get-tuple-element.7) | data formatting | bytes 262144
  (6 shorter events, 0.1 us)
Async XLA Ops:
  0.6 0.7 copy-start

commit v2 on v1

--- a/solution.py
+++ b/solution.py
@@ -29,11 +29,10 @@
     w_gate,
     w_up,
     w_down,
-    slots,
-    final_gain,
+    slab_of,
     order,
     stream_out,
-    normed_out,
+    factor_out,
     ow,
     wg,
     wu,
@@ -64,7 +63,9 @@
     y, c = t // 2, t % 2
     rows, dl = residual.shape
     d_model = dl * parts
-    count = router.shape[1]
+    count = router.shape[0]
+    slab_count = groups // count
+    chunks, _, wide = slab.shape
     fl = act.shape[1]
     half = fl // 2
     slots_all = groups * MOST
@@ -139,18 +140,32 @@
             wd_copies.append(cp)
             n += 1
 
-    route_f = routes[...].astype(F32)
+    ri = lax.broadcasted_iota(jnp.int32, (rows, rows), 0)
+    ci = lax.broadcasted_iota(jnp.int32, (rows, rows), 1)
+    same = jnp.where(ci == ri, 1.0, 0.0).astype(BF)
+    route_f = lax.dot_general(
+        same,
+        routes[...].astype(F32).astype(BF),
+        (((1,), (1,)), ((), ())),
+        preferred_element_type=F32,
+    )
+    column = lax.broadcasted_iota(jnp.int32, (1, slots_all), 1)
+    held = jnp.zeros((1, slots_all), F32)
+    slot = column
+    for o in range(groups):
+        expert = lax.div(slab_of[lax.rem(e + o, groups)], slab_count).astype(F32)
+        held = jnp.where(column >= o * MOST, expert, held)
+        slot = jnp.where(column >= o * MOST, column - o * MOST, slot)
+    slot = slot.astype(F32)
     ids = lax.broadcasted_iota(jnp.int32, (rows, count), 1).astype(F32)
     hot = [jnp.where(route_f[:, k : k + 1] == ids, 1.0, 0.0) for k in range(2)]
-    ri = lax.broadcasted_iota(jnp.int32, (rows, rows), 0)
-    ci = lax.broadcasted_iota(jnp.int32, (rows, rows), 1)
     lower = jnp.where(ci < ri, 1.0, 0.0).astype(BF)
     before = dot(lower, (hot[0] + hot[1]).astype(BF))
     sel = []
     for k in range(2):
         place = jnp.sum(hot[k] * before, axis=1, keepdims=True)
-        hit = jnp.where(slots[0:1, :] == route_f[:, k : k + 1], 1.0, 0.0)
-        fit = jnp.where(slots[1:2, :] == place, 1.0, 0.0)
+        hit = jnp.where(held == route_f[:, k : k + 1], 1.0, 0.0)
+        fit = jnp.where(slot == place, 1.0, 0.0)
         sel.append(hit * fit)
     placing = (sel[0] + sel[1]).astype(BF)
     sel = [s.astype(BF) for s in sel]
@@ -163,8 +178,12 @@
     hidden = (residual[...].astype(F32) + own).astype(BF).astype(F32)
     scaled = hidden * gain[...]
     stat_send[...] = jnp.zeros_like(stat_send)
-    stat_send[:, 0:count] = jnp.dot(
-        scaled, router[...], precision=lax.Precision.HIGHEST, preferred_element_type=F32
+    stat_send[:, 0:count] = lax.dot_general(
+        scaled,
+        router[...],
+        (((1,), (1,)), ((), ())),
+        precision=lax.Precision.HIGHEST,
+        preferred_element_type=F32,
     )
     stat_send[:, count : count + 1] = jnp.sum(hidden * hidden, axis=1, keepdims=True)
     stat_copies = []
@@ -194,22 +213,38 @@
         cp.start()
         out_copies.append(cp)
     arr[0, 0:MOST] = out_rows[0:MOST]
-    for cp in out_copies:
-        cp.wait_recv()
-
-    spread = [remote(arr.at[0], arr.at[2 * yo], at_part(2 * yo)) for yo in range(1, ny)]
-    spread_sib = remote(arr.at[0], arr.at[1], at_part(1))
-    for cp in spread:
-        cp.start()
-    spread_sib.start()
-    passed = []
-    for yo in range(1, ny):
-        spread[yo - 1].wait_recv()
-        cp = remote(arr.at[2 * yo], arr.at[2 * yo + 1], at_part(1))
-        cp.start()
-        passed.append(cp)
-    spread_sib.wait_recv()
-    for cp in passed:
+    pieces = 4 if groups % 4 == 0 else 1
+    per = groups // pieces
+    spread, waiting = [], []
+
+    def forward():
+        for cp in waiting.pop(0):
+            cp[0].wait_recv()
+            cp[1].start()
+            spread.append(cp[1])
+
+    last = []
+    for q in range(pieces):
+        for o in range(max(q * per, 1), (q + 1) * per):
+            out_copies[o - 1].wait_recv()
+        block = pl.ds(q * per * MOST, per * MOST)
+        pairs = []
+        for yo in range(1, ny):
+            cp = remote(arr.at[0, block], arr.at[2 * yo, block], at_part(2 * yo))
+            cp.start()
+            spread.append(cp)
+            on = remote(arr.at[2 * yo, block], arr.at[2 * yo + 1, block], at_part(1))
+            pairs.append((cp, on))
+            last.append(on)
+        cp = remote(arr.at[0, block], arr.at[1, block], at_part(1))
+        cp.start()
+        spread.append(cp)
+        last.append(cp)
+        waiting.append(pairs)
+        if q:
+            forward()
+    forward()
+    for cp in last:
         cp.wait_recv()
     for cp in gu_copies:
         cp.wait()
@@ -233,69 +268,107 @@
 
     for cp in wd_copies:
         cp.wait()
-    dc = min(256, dl)
-
-    def down(j):
+    dc = min(256, wide)
+
+    def down(j, f):
         @pl.loop(0, slots_all // rc)
         def _(r):
             rr = pl.ds(pl.multiple_of(r * rc, rc), rc)
 
-            @pl.loop(0, dl // dc)
-            def _(f):
-                cc = pl.ds(pl.multiple_of(f * dc, dc), dc)
+            @pl.loop(0, wide // dc)
+            def _(n):
+                to = pl.ds(pl.multiple_of(n * dc, dc), dc)
+                cc = pl.ds(pl.multiple_of(f * wide + n * dc, dc), dc)
                 value = dot(act[rr, 0:half], wd[j, :, cc])
                 value += dot(act[rr, half:fl], ow[j, 0:half, cc])
-                part[j, rr, cc] = value.astype(BF)
-
-    sib_copies = []
+                part[f, j, rr, to] = value.astype(BF)
+
+    sib_copies, cross, back, moved = [], [], [], []
     yos = list(range(1, ny)) + [0]
-    for yo in yos:
-        down(2 * yo + 1)
-        cp = remote(part.at[2 * yo + 1], sib.at[yo], at_part(1))
-        cp.start()
-        sib_copies.append(cp)
-    cross = []
-    for n, yo in enumerate(yos):
-        down(2 * yo)
-        sib_copies[n].wait_recv()
-        if yo:
-            cross_send[yo - 1] = (part[2 * yo].astype(F32) + sib[yo].astype(F32)).astype(BF)
-            cp = remote(cross_send.at[yo - 1], cross_recv.at[yo - 1], at_part(2 * yo))
-            cp.start()
-            cross.append(cp)
-    for cp in cross:
+    crossing = []
+    for f in range(chunks):
+        mine = []
+        for yo in yos:
+            down(2 * yo + 1, f)
+            cp = remote(part.at[f, 2 * yo + 1], sib.at[f, yo], at_part(1))
+            cp.start()
+            mine.append(cp)
+        sib_copies += mine
+        row = []
+        for n, yo in enumerate(yos):
+            down(2 * yo, f)
+            mine[n].wait_recv()
+            if yo:
+                cross_send[f, yo - 1] = (
+                    part[f, 2 * yo].astype(F32) + sib[f, yo].astype(F32)
+                ).astype(BF)
+                cp = remote(cross_send.at[f, yo - 1], cross_recv.at[f, yo - 1], at_part(2 * yo))
+                cp.start()
+                row.append(cp)
+        crossing.append(row)
+        cross += row
+
+    returning = []
+    for f in range(chunks):
+        total = part[f, 0].astype(F32) + sib[f, 0].astype(F32)
+        for yo in range(1, ny):
+            crossing[f][yo - 1].wait_recv()
+            total = total + cross_recv[f, yo - 1].astype(F32)
+        slab[f] = total.astype(BF)
+        row = []
+        for o in range(1, groups):
+            block = pl.ds(o * MOST, MOST)
+            cp = remote(slab.at[f, block], ret.at[f, block], at_group(o, -1))
+            cp.start()
+            row.append(cp)
+        ret[f, 0:MOST] = slab[f, 0:MOST]
+        returning.append(row)
+        back += row
+
+    side = lax.rem(e, 2)
+    pair = e // 2
+    pairs_all = groups // 2
+    partner = (e + 1 - 2 * side, t)
+
+    def block_of(device):
+        return pl.ds(pl.multiple_of(device * rows, rows), rows)
+
+    first_hop, second_hop = [], []
+    for f in range(chunks):
+        for cp in returning[f]:
+            cp.wait_recv()
+        blended = mixing[0] * dot(sel[0], ret[f]) + mixing[1] * dot(sel[1], ret[f])
+        own_rows = block_of(e)
+        all_stream[f, own_rows] = (hidden[:, f * wide : (f + 1) * wide] + blended).astype(BF)
+        row = []
+        for o in range(1, pairs_all):
+            to = lax.rem(pair + o, pairs_all) * 2 + side
+            cp = remote(all_stream.at[f, own_rows], all_stream.at[f, own_rows], (to, t))
+            cp.start()
+            row.append(cp)
+        cp = remote(all_stream.at[f, own_rows], all_stream.at[f, own_rows], partner)
+        cp.start()
+        second_hop.append(cp)
+        first_hop.append(row)
+        moved += row + [cp]
+    for f in range(chunks):
+        for o in range(1, pairs_all):
+            first_hop[f][o - 1].wait_recv()
+            source = block_of(lax.rem(pair - o + pairs_all, pairs_all) * 2 + side)
+            cp = remote(all_stream.at[f, source], all_stream.at[f, source], partner)
+            cp.start()
+            second_hop.append(cp)
+            moved.append(cp)
+    want = lax.broadcasted_iota(jnp.int32, (rows, groups * rows), 0)
+    pick = jnp.where(order[...] - e * rows == want, 1.0, 0.0).astype(BF)
+    for cp in second_hop:
         cp.wait_recv()
-    total = part[0].astype(F32) + sib[0].astype(F32)
-    for yo in range(1, ny):
-        total = total + cross_recv[yo - 1].astype(F32)
-    slab[...] = total.astype(BF)
-
-    back = []
-    for o in range(1, groups):
-        part_rows = pl.ds(o * MOST, MOST)
-        cp = remote(slab.at[part_rows], ret.at[part_rows], at_group(o, -1))
-        cp.start()
-        back.append(cp)
-    ret[0:MOST] = slab[0:MOST]
-    for cp in back:
-        cp.wait_recv()
-    blended = mixing[0] * dot(sel[0], ret[...]) + mixing[1] * dot(sel[1], ret[...])
-    all_stream[0:rows] = (hidden + blended).astype(BF)
-
-    moved = []
-    for o in range(1, groups):
-        cp = remote(
-            all_stream.at[pl.ds(0, rows)], all_stream.at[pl.ds(o * rows, rows)], at_group(o)
-        )
-        cp.start()
-        moved.append(cp)
-    want = lax.broadcasted_iota(jnp.int32, (rows, groups * rows), 0).astype(F32)
-    pick = jnp.where(order[...] == want, 1.0, 0.0).astype(BF)
-    for cp in moved:
-        cp.wait_recv()
-    stream = dot(pick, all_stream[...])
-    stream_out[...] = stream.astype(BF)
-    sq_send[...] = jnp.broadcast_to(jnp.sum(stream * stream, axis=1, keepdims=True), sq_send.shape)
+    squares = jnp.zeros((rows, 1), F32)
+    for f in range(chunks):
+        stream = dot(pick, all_stream[f])
+        stream_out[:, f * wide : (f + 1) * wide] = stream
+        squares = squares + jnp.sum(stream * stream, axis=1, keepdims=True)
+    sq_send[...] = jnp.broadcast_to(squares, sq_send.shape)
     sq_copies = []
     for j in range(1, parts):
         cp = remote(sq_send, sq_recv.at[j - 1], at_part(j))
@@ -306,10 +379,9 @@
         cp.wait_recv()
     for j in range(parts - 1):
         square = square + sq_recv[j]
-    factor = lax.rsqrt(square[:, 0:1] / d_model + EPS)
-    normed_out[...] = (stream * factor * final_gain[...]).astype(BF)
-
-    started = proj_copies + stat_copies + out_copies + spread + [spread_sib] + passed
+    factor_out[...] = lax.rsqrt(square / d_model + EPS)
+
+    started = proj_copies + stat_copies + out_copies + spread
     for cp in started + sib_copies + cross + back + moved + sq_copies:
         cp.wait_send()
 
@@ -331,28 +403,27 @@
     groups = lax.axis_size("expert")
     parts = lax.axis_size("tensor")
     ny = parts // 2
-    e = lax.axis_index("expert")
     rows, dl = residual.shape
     d_model = out_weight.shape[1]
-    slab_count = groups // router_weight.shape[1]
     fl = w_gate.shape[2]
     slots_all = groups * MOST
-    steps = jnp.arange(groups, dtype=jnp.int32)
-    held = jnp.take(slab_of // slab_count, (e + steps) % groups)
-    slots = jnp.stack(
-        [jnp.repeat(held, MOST), jnp.arange(slots_all, dtype=jnp.int32) % MOST]
-    ).astype(F32)
-    order = jnp.take(row_order.reshape(groups, rows), (e - steps) % groups, axis=0)
-    order = (order.reshape(1, groups * rows) - e * rows).astype(F32)
+    wide = 512 if dl % 512 == 0 else dl
+    chunks = dl // wide
+    pieces = 4 if groups % 4 == 0 else 1
     vmem = pl.BlockSpec(memory_space=pltpu.VMEM)
     hbm = pl.BlockSpec(memory_space=pl.ANY)
-    copies = 3 * (parts - 1) + 3 * (groups - 1) + 2 * (ny - 1) + 1 + ny + ny - 1
+    smem = pl.BlockSpec(memory_space=pltpu.SMEM)
+    copies = 3 * (parts - 1) + groups - 1 + pieces * (2 * ny - 1)
+    copies += chunks * (2 * ny - 1 + 2 * (groups - 1))
     flops = 2 * (rows * dl * d_model + 3 * slots_all * d_model * fl)
     moved = 2 * (dl * d_model + 3 * d_model * fl)
     call = pl.pallas_call(
         functools.partial(layer_kernel, groups, parts),
-        out_shape=[jax.ShapeDtypeStruct((rows, dl), BF)] * 2,
-        in_specs=[vmem, vmem, hbm, vmem, vmem, vmem, hbm, hbm, hbm, vmem, vmem, vmem],
+        out_shape=[
+            jax.ShapeDtypeStruct((rows, dl), F32),
+            jax.ShapeDtypeStruct((rows, 128), F32),
+        ],
+        in_specs=[vmem, vmem, hbm, vmem, vmem, vmem, hbm, hbm, hbm, smem, vmem],
         out_specs=[vmem, vmem],
         scratch_shapes=[
             pltpu.VMEM((parts, dl, dl), BF),
@@ -366,13 +437,13 @@
             pltpu.VMEM((slots_all, dl), BF),
             pltpu.VMEM((parts, slots_all, dl), BF),
             pltpu.VMEM((slots_all, fl), BF),
-            pltpu.VMEM((parts, slots_all, dl), BF),
-            pltpu.VMEM((ny, slots_all, dl), BF),
-            pltpu.VMEM((max(ny - 1, 1), slots_all, dl), BF),
-            pltpu.VMEM((max(ny - 1, 1), slots_all, dl), BF),
-            pltpu.VMEM((slots_all, dl), BF),
-            pltpu.VMEM((slots_all, dl), BF),
-            pltpu.VMEM((groups * rows, dl), BF),
+            pltpu.VMEM((chunks, parts, slots_all, wide), BF),
+            pltpu.VMEM((chunks, ny, slots_all, wide), BF),
+            pltpu.VMEM((chunks, max(ny - 1, 1), slots_all, wide), BF),
+            pltpu.VMEM((chunks, max(ny - 1, 1), slots_all, wide), BF),
+            pltpu.VMEM((chunks, slots_all, wide), BF),
+            pltpu.VMEM((chunks, slots_all, wide), BF),
+            pltpu.VMEM((chunks, groups * rows, wide), BF),
             pltpu.VMEM((rows, 128), F32),
             pltpu.VMEM((parts - 1, rows, 128), F32),
             pltpu.SemaphoreType.DMA((5 * parts,)),
@@ -384,20 +455,21 @@
         ),
         cost_estimate=pl.CostEstimate(flops=flops, bytes_accessed=moved, transcendentals=0),
     )
-    return call(
+    stream, factor = call(
         attn_vals,
         residual,
         out_weight,
         norm_gain.reshape(1, dl),
-        router_weight,
-        routes,
+        router_weight.T,
+        routes.T,
         w_gate,
         w_up,
         w_down,
-        slots,
-        final_gain.reshape(1, dl),
-        order,
+        slab_of,
+        row_order.reshape(1, groups * rows),
     )
+    normed = stream * factor[:, 0:1] * final_gain[None, :]
+    return stream.astype(BF), normed.astype(BF)
 
 
 def solution(mesh):

time: 132 us -> 97 us (0.73)
  Pallas kernels: 120 us -> 92 us
  local copies, waits for them, and re-layouts: 9.61 us -> 0.87 us
    pallas_call x1, Pallas kernels: 120 us -> 92 us  [on_device(): call(attn_vals, residual, out_weight, norm_gain.reshape(1, dl), router_we...]
    unnamed x6 -> x2, local copies, waits for them, and re-layouts: 6.86 us -> 0.01 us
where the time goes in v2:
time: 97 us; the launch traced here: 95.3 us
  Pallas kernels  92 us (95%)
  other arithmetic  1.78 us (2%)
    pallas_call x1, Pallas kernels, on_device(): call(attn_vals, residual, out_weight, norm_gain.reshape(1, dl), router_we...  92 us

profile of v2, /device:TPU:27, one launch (start us, length us, event | category | flops | bytes accessed | tf_op | source)
XLA Modules:
  0.0 95.3 jit_solution(18311582123170113827)
XLA Ops:
  0.6 0.0 copy-start
  0.6 92.0 %shard_map.131 = (f32[64,1024]{1,0:T(8,128)}, f32[64,128]{1,0:T(8,128)}) custom-call(bf16[64,1024]{1,0:T(8,128)(2,1)} %attn.1, bf16[64,1024]{1,0:T(8,128)(2,1)} %residual.1, bf16[1024,4096]{1,0:T(8,128)(2,1)} %out_w.1, f32[1,1024]{1,0:T(1,128)} %bitcast.5, f32[8,1024]{1,0:T(8,128)} %bitcast.4, s32[2,64]{1,0:T(2,128)} %bitcast.7, ...), custom_call_target="tpu_custom_call" | custom-call | flops 13421772800 | bytes 58720256 | tf_op jit(solution)/shard_map/pallas_call | solution.py:458
  92.7 0.9 slice_reduce_fusion
  93.6 0.0 copy-done
  93.6 1.8 %multiply_convert_fusion = (bf16[64,1024]{1,0:T(8,128)(2,1)}, bf16[64,1024]{1,0:T(8,128)(2,1)}) fusion(f32[64,1024]{1,0:T(8,128)} %get-tuple-element.4, f32[1024]{0:T(1024)S(1)} %copy-done, f32[64]{0:T(128)S(1)} %slice_reduce_fusion), kind=kLoop, calls=%fused_computation | loop fusion | flops 262144 | bytes 528640 | tf_op jit(solution)/shard_map/convert_element_type | solution.py:472
Async XLA Ops:
  0.6 92.9 %copy-start = (f32[1024]{0:T(1024)S(1)}, f32[1024]{0:T(1024)}, u32[]{:S(2)}) copy-start(f32[1024]{0:T(1024)} %param.22) | copy-start | bytes 12292

commit v3 on v2

--- a/solution.py
+++ b/solution.py
@@ -31,8 +31,9 @@
     w_down,
     slab_of,
     order,
+    final_gain,
     stream_out,
-    factor_out,
+    normed_out,
     ow,
     wg,
     wu,
@@ -379,7 +380,8 @@
         cp.wait_recv()
     for j in range(parts - 1):
         square = square + sq_recv[j]
-    factor_out[...] = lax.rsqrt(square / d_model + EPS)
+    factor = lax.rsqrt(square[:, 0:1] / d_model + EPS)
+    normed_out[...] = stream_out[...] * factor * final_gain[...]
 
     started = proj_copies + stat_copies + out_copies + spread
     for cp in started + sib_copies + cross + back + moved + sq_copies:
@@ -407,7 +409,7 @@
     d_model = out_weight.shape[1]
     fl = w_gate.shape[2]
     slots_all = groups * MOST
-    wide = 512 if dl % 512 == 0 else dl
+    wide = 256 if dl % 256 == 0 else dl
     chunks = dl // wide
     pieces = 4 if groups % 4 == 0 else 1
     vmem = pl.BlockSpec(memory_space=pltpu.VMEM)
@@ -419,11 +421,8 @@
     moved = 2 * (dl * d_model + 3 * d_model * fl)
     call = pl.pallas_call(
         functools.partial(layer_kernel, groups, parts),
-        out_shape=[
-            jax.ShapeDtypeStruct((rows, dl), F32),
-            jax.ShapeDtypeStruct((rows, 128), F32),
-        ],
-        in_specs=[vmem, vmem, hbm, vmem, vmem, vmem, hbm, hbm, hbm, smem, vmem],
+        out_shape=[jax.ShapeDtypeStruct((rows, dl), F32)] * 2,
+        in_specs=[vmem, vmem, hbm, vmem, vmem, vmem, hbm, hbm, hbm, smem, vmem, vmem],
         out_specs=[vmem, vmem],
         scratch_shapes=[
             pltpu.VMEM((parts, dl, dl), BF),
@@ -455,7 +454,7 @@
         ),
         cost_estimate=pl.CostEstimate(flops=flops, bytes_accessed=moved, transcendentals=0),
     )
-    stream, factor = call(
+    stream, normed = call(
         attn_vals,
         residual,
         out_weight,
@@ -467,8 +466,8 @@
         w_down,
         slab_of,
         row_order.reshape(1, groups * rows),
+        final_gain.reshape(1, dl),
     )
-    normed = stream * factor[:, 0:1] * final_gain[None, :]
     return stream.astype(BF), normed.astype(BF)
 
 

time: 97 us -> 98.1 us (1.011); the launches traced: 95.3 us -> 97.8 us
  Pallas kernels: 92 us -> 93.9 us
  other arithmetic: 1.78 us -> 3.24 us
    pallas_call x1, Pallas kernels: 92 us -> 93.9 us  [on_device(): call(attn_vals, residual, out_weight, norm_gain.reshape(1, dl), router_we...]
    convert_element_type x1 -> x2, other arithmetic: 1.78 us -> 3.24 us  [on_device(): return (stream.astype(BF), normed.astype(BF))]
where the time goes in v3:
time: 98.1 us; the launch traced here: 97.8 us
  Pallas kernels  93.9 us (96%)
  other arithmetic  3.24 us (3%)
    pallas_call x1, Pallas kernels, on_device(): call(attn_vals, residual, out_weight, norm_gain.reshape(1, dl), router_we...  93.9 us
    convert_element_type x2, other arithmetic, on_device(): return (stream.astype(BF), normed.astype(BF))  3.24 us

profile of v3, /device:TPU:27, one launch (start us, length us, event | category | flops | bytes accessed | tf_op | source)
XLA Modules:
  0.0 97.8 jit_solution(6133264441199597718)
XLA Ops:
  0.6 93.9 %shard_map.131 = (f32[64,1024]{1,0:T(8,128)}, f32[64,1024]{1,0:T(8,128)}) custom-call(bf16[64,1024]{1,0:T(8,128)(2,1)} %attn.1, bf16[64,1024]{1,0:T(8,128)(2,1)} %residual.1, bf16[1024,4096]{1,0:T(8,128)(2,1)} %out_w.1, f32[1,1024]{1,0:T(1,128)} %bitcast.6, f32[8,1024]{1,0:T(8,128)} %bitcast.5, s32[2,64]{1,0:T(2,128)} %bitcast.9, ...), custom_call_target="tpu_custom_call" | custom-call | flops 13421772800 | bytes 58720256 | tf_op jit(solution)/shard_map/pallas_call | solution.py:457
  94.6 1.6 %convert_element_type.6 = bf16[64,1024]{1,0:T(8,128)(2,1)} convert(f32[64,1024]{1,0:T(8,128)} %get-tuple-element.4) | non-fusion elementwise | flops 65536 | bytes 393216 | tf_op jit(solution)/shard_map/convert_element_type | solution.py:471
  96.2 1.6 %convert_element_type.7 = bf16[64,1024]{1,0:T(8,128)(2,1)} convert(f32[64,1024]{1,0:T(8,128)} %get-tuple-element.5) | non-fusion elementwise | flops 65536 | bytes 393216 | tf_op jit(solution)/shard_map/convert_element_type | solution.py:471
